TPU v7x, 32 devices: a whole 2x2x4 slice. The times are simulated.
32 devices in a mesh: ctx: 4 (over x, core), tp: 8 (over z, y).
Axes of the slice: x: 2, y: 2, z: 4, core: 2. Of those that a mesh axis runs over, the one named last changes fastest.
Arguments:
- streams: bfloat16 [3, 4096, 8192], P(None, 'ctx', 'tp'), may hold values from -6 to 6
- conv_weight: float32 [3, 3, 8192], P(None, None, 'tp'), may hold values from -3.5 to 3.5
- skip_weight: float32 [8192], P('tp'), may hold values from -4 to 4
- long_filter: bfloat16 [4096, 8192], P('ctx', 'tp'), may hold values from -1.6 to 1.6
- out_weight: bfloat16 [8192, 8192], P('tp'), may hold values from -0.09375 to 0.09375
Outputs:
- projected: bfloat16 [4096, 8192], P('ctx', 'tp')
All inputs are finite; a program needn't handle non-finite values.
Results may differ from a plain program's by a relative error of at most 0.015.
Values may be sent and summed in bfloat16 or wider, within the bound.
No kernel may reach another device: no remote copies, remote signals or barrier semaphores. Data moves between devices by JAX's collectives and lax.ppermute only.
A program may use at most 192 MiB of HBM per device.

v0:
```python
import math

import jax
import jax.numpy as jnp
from jax import lax
from jax.sharding import PartitionSpec as P

three_pass = lax.Precision.HIGH


def shifted(value, axis, steps):
    count = lax.axis_size(axis)
    initial, last = (max(0, -steps), min(count, count - steps))
    return lax.ppermute(value, axis, [(source, source + steps) for source in range(initial, last)])


def fft_conv(signal, kernel):
    seq_len, chan_count = signal.shape
    full_len = 2 * seq_len
    col_count = 128
    row_count = full_len // col_count
    half_rows = row_count // 2
    row_index = lax.iota(jnp.int32, row_count)
    half_index = lax.iota(jnp.int32, half_rows)
    col_index = lax.iota(jnp.int32, col_count)
    angle_rows = (row_index[:, None] * half_index[None, :] % row_count).astype(jnp.float32) * (
        2.0 * math.pi / row_count
    )
    cos_rows = jnp.cos(angle_rows)
    sin_rows = jnp.sin(angle_rows)
    angle_twist = (row_index[:, None] * col_index[None, :] % full_len).astype(jnp.float32) * (
        2.0 * math.pi / full_len
    )
    cos_twist = jnp.cos(angle_twist)
    sin_twist = jnp.sin(angle_twist)
    angle_cols = (col_index[:, None] * col_index[None, :] % col_count).astype(jnp.float32) * (
        2.0 * math.pi / col_count
    )
    cos_cols = jnp.cos(angle_cols)
    sin_cols = jnp.sin(angle_cols)

    def forward(field):
        re_first = jnp.einsum("an,cnm->cam", cos_rows, field, precision=three_pass)
        im_first = -jnp.einsum("an,cnm->cam", sin_rows, field, precision=three_pass)
        re_twist = re_first * cos_twist + im_first * sin_twist
        im_twist = im_first * cos_twist - re_first * sin_twist
        re_spec = jnp.einsum("cam,mk->cak", re_twist, cos_cols, precision=three_pass) + jnp.einsum(
            "cam,mk->cak", im_twist, sin_cols, precision=three_pass
        )
        im_spec = jnp.einsum("cam,mk->cak", im_twist, cos_cols, precision=three_pass) - jnp.einsum(
            "cam,mk->cak", re_twist, sin_cols, precision=three_pass
        )
        return (re_spec, im_spec)

    sig_field = signal.astype(jnp.float32).T.reshape(chan_count, half_rows, col_count)
    ker_field = kernel.astype(jnp.float32).T.reshape(chan_count, half_rows, col_count)
    re_sig, im_sig = forward(sig_field)
    re_ker, im_ker = forward(ker_field)
    re_prod = re_sig * re_ker - im_sig * im_ker
    im_prod = re_sig * im_ker + im_sig * re_ker
    re_back = jnp.einsum("cak,mk->cam", re_prod, cos_cols, precision=three_pass) - jnp.einsum(
        "cak,mk->cam", im_prod, sin_cols, precision=three_pass
    )
    im_back = jnp.einsum("cak,mk->cam", im_prod, cos_cols, precision=three_pass) + jnp.einsum(
        "cak,mk->cam", re_prod, sin_cols, precision=three_pass
    )
    re_untwist = re_back * cos_twist - im_back * sin_twist
    im_untwist = im_back * cos_twist + re_back * sin_twist
    output_field = jnp.einsum(
        "an,cam->cnm", cos_rows, re_untwist, precision=three_pass
    ) - jnp.einsum("an,cam->cnm", sin_rows, im_untwist, precision=three_pass)
    output_field = output_field * (1.0 / full_len)
    return output_field.reshape(chan_count, seq_len).T


def on_device(streams, conv_weight, skip_weight, long_filter, out_weight):
    tok_rows = streams.shape[1]
    chan_cols = streams.shape[2]
    tap_count = conv_weight.shape[1]
    rim_rows = shifted(streams[:, tok_rows - (tap_count - 1) :, :], "ctx", 1)
    extended = jnp.concatenate([rim_rows, streams], axis=1).astype(jnp.float32)
    summed = jnp.zeros((3, tok_rows, chan_cols), jnp.float32)
    for lag_step in range(tap_count):
        begin = tap_count - 1 - lag_step
        summed = (
            summed + conv_weight[:, lag_step, None, :] * extended[:, begin : begin + tok_rows, :]
        )
    gating = summed[0]
    mixed_u = (summed[1] * summed[2]).astype(jnp.bfloat16)
    groups = lax.axis_size("ctx")
    group_width = chan_cols // groups
    mixed_three = mixed_u.reshape(tok_rows, groups, group_width)
    filter_three = long_filter.reshape(tok_rows, groups, group_width)
    signal_full = lax.all_to_all(mixed_three, "ctx", split_axis=1, concat_axis=0, tiled=True)
    kernel_full = lax.all_to_all(filter_three, "ctx", split_axis=1, concat_axis=0, tiled=True)
    long_part = fft_conv(signal_full[:, 0, :], kernel_full[:, 0, :]).astype(jnp.bfloat16)[
        :, None, :
    ]
    long_three = lax.all_to_all(long_part, "ctx", split_axis=0, concat_axis=1, tiled=True)
    long_out = long_three.reshape(tok_rows, chan_cols)
    gated = (
        (long_out.astype(jnp.float32) + skip_weight[None, :] * mixed_u.astype(jnp.float32)) * gating
    ).astype(jnp.bfloat16)
    result = lax.psum_scatter(
        lax.dot_general(
            out_weight, gated, (((0,), (1,)), ((), ())), preferred_element_type=jnp.float32
        ),
        "tp",
        scatter_dimension=0,
        tiled=True,
    ).T
    return result.astype(jnp.bfloat16)


def solution(mesh):
    return jax.shard_map(
        on_device,
        mesh=mesh,
        in_specs=(
            P(None, "ctx", "tp"),
            P(None, None, "tp"),
            P("tp"),
            P("ctx", "tp"),
            P("tp", None),
        ),
        out_specs=P("ctx", "tp"),
        check_vma=False,
    )
```

profile of v0, /device:TPU:0, one launch (start us, length us, event | category | flops | bytes accessed | tf_op | source)
XLA Modules:
  0.0 932.7 jit_solution(6282414886590193314)
XLA Ops:
  15.2 4.4 all-to-all-start.1
  19.8 8.7 copy.75
  29.0 11.0 %maximum_convert_fusion = f32[3,1026,1024]{1,2,0:T(8,128)} fusion(bf16[3,1024,1024]{1,2,0:T(8,128)(2,1)} %copy.75, bf16[3,2,1024]{1,2,0:T(8,128)(2,1)S(1)} %copy.74), kind=kLoop, calls=%fused_computation.48 | loop fusion | flops 12607488 | bytes 18911232 | tf_op jit(solution)/shard_map/convert_element_type | solution.py:81
  40.0 18.2 %fusion = f32[3,1024,1024]{1,2,0:T(8,128)S(1)} fusion(f32[3,1026,1024]{1,2,0:T(8,128)} %maximum_convert_fusion, f32[3,1024]{1,0:T(4,128)S(1)} %get-tuple-element.14, f32[3,1024]{1,0:T(4,128)S(1)} %get-tuple-element.15, f32[3,1024]{1,0:T(4,128)S(1)} %bitcast.133), kind=kLoop, calls=%fused_computation.2 | loop fusion | flops 15728640 | bytes 50368512 | tf_op jit(solution)/shard_map/add | solution.py:86
  58.2 4.5 copy-done
  66.0 4.4 all-to-all-start
  70.6 4.1 copy.82
  79.2 4.4 add_bitcast_fusion
  83.6 12.8 %fusion.24 = f32[256,64,128]{2,0,1:T(8,128)} fusion(f32[256,64,128]{2,1,0:T(8,128)S(1)} %get-tuple-element.9), kind=kOutput, calls=%fused_computation.36 | convolution fusion | flops 1610842112 | bytes 16777216 | tf_op jit(solution)/shard_map/cam,mk->cak/dot_general | solution.py:50
  96.5 12.6 %fusion.26 = f32[256,64,128]{2,0,1:T(8,128)} fusion(f32[256,64,128]{2,1,0:T(8,128)S(1)} %get-tuple-element.9), kind=kOutput, calls=%fused_computation.38 | convolution fusion | flops 1610842112 | bytes 16777216 | tf_op jit(solution)/shard_map/cam,mk->cak/dot_general | solution.py:47
  109.0 12.9 %fusion.22 = f32[256,64,128]{2,0,1:T(8,128)} fusion(f32[256,64,128]{2,1,0:T(8,128)S(1)} %get-tuple-element.10), kind=kOutput, calls=%fused_computation.34 | convolution fusion | flops 1610842112 | bytes 16777216 | tf_op jit(solution)/shard_map/cam,mk->cak/dot_general | solution.py:47
  122.0 2.9 copy.77
  129.2 5.8 fusion.2
  135.0 12.8 %fusion.32 = f32[256,64,128]{2,0,1:T(8,128)} fusion(f32[256,64,128]{2,1,0:T(8,128)S(1)} %get-tuple-element.7), kind=kOutput, calls=%fused_computation.44 | convolution fusion | flops 1610842112 | bytes 16777216 | tf_op jit(solution)/shard_map/cam,mk->cak/dot_general | solution.py:50
  147.8 12.5 %fusion.34 = f32[256,64,128]{2,0,1:T(8,128)} fusion(f32[256,64,128]{2,1,0:T(8,128)S(1)} %get-tuple-element.7), kind=kOutput, calls=%fused_computation.46 | convolution fusion | flops 1610842112 | bytes 16777216 | tf_op jit(solution)/shard_map/cam,mk->cak/dot_general | solution.py:47
  160.3 12.8 %fusion.28 = f32[256,64,128]{2,0,1:T(8,128)} fusion(f32[256,64,128]{2,1,0:T(8,128)S(1)} %get-tuple-element.8), kind=kOutput, calls=%fused_computation.40 | convolution fusion | flops 1610842112 | bytes 16777216 | tf_op jit(solution)/shard_map/cam,mk->cak/dot_general | solution.py:50
  173.1 12.6 %fusion.30 = f32[256,64,128]{2,0,1:T(8,128)} fusion(f32[256,64,128]{2,1,0:T(8,128)S(1)} %get-tuple-element.8), kind=kOutput, calls=%fused_computation.42 | convolution fusion | flops 1610842112 | bytes 16777216 | tf_op jit(solution)/shard_map/cam,mk->cak/dot_general | solution.py:47
  185.6 31.0 %multiply_subtract_fusion = (f32[256,64,128]{2,0,1:T(8,128)}, f32[256,64,128]{2,0,1:T(8,128)}) fusion(f32[256,64,128]{2,0,1:T(8,128)} %fusion.24, f32[256,64,128]{2,0,1:T(8,128)} %fusion.28, f32[256,64,128]{2,0,1:T(8,128)} %fusion.32, f32[256,64,128]{2,0,1:T(8,128)} %fusion.26, f32[256,64,128]{2,0,1:T(8,128)} %fusion.22, f32[256,64,128]{2,0,1:T(8,128)} %fusion.34, ...), kind=kOutput, calls=%fused_computation.21 | convolution fusion | flops 1631813632 | bytes 83886080 | tf_op jit(solution)/shard_map/cam,mk->cak/dot_general | solution.py:50
  216.6 13.9 %fusion.16 = f32[256,64,128]{2,1,0:T(8,128)S(1)} fusion(f32[256,64,128]{2,0,1:T(8,128)} %get-tuple-element.5), kind=kOutput, calls=%fused_computation.28 | convolution fusion | flops 1610842112 | bytes 16777216 | tf_op jit(solution)/shard_map/cak,mk->cam/dot_general | solution.py:64
  230.6 9.7 %fusion.18 = f32[256,64,128]{2,1,0:T(8,128)} fusion(f32[256,64,128]{2,0,1:T(8,128)S(1)} %copy-done.2), kind=kOutput, calls=%fused_computation.30 | convolution fusion | flops 1610842112 | bytes 16777216 | tf_op jit(solution)/shard_map/cak,mk->cam/dot_general | solution.py:61
  240.3 9.6 %fusion.12 = f32[256,64,128]{2,1,0:T(8,128)} fusion(f32[256,64,128]{2,0,1:T(8,128)S(1)} %bitcast.122), kind=kOutput, calls=%fused_computation.24 | convolution fusion | flops 1610842112 | bytes 16777216 | tf_op jit(solution)/shard_map/cak,mk->cam/dot_general | solution.py:64
  249.9 9.7 %fusion.14 = f32[256,64,128]{2,1,0:T(8,128)} fusion(f32[256,64,128]{2,0,1:T(8,128)S(1)} %bitcast.122), kind=kOutput, calls=%fused_computation.26 | convolution fusion | flops 1610842112 | bytes 16777216 | tf_op jit(solution)/shard_map/cak,mk->cam/dot_general | solution.py:61
  259.6 14.6 %fusion.4 = f32[256,128,32]{1,2,0:T(8,128)} fusion(f32[64,128]{1,0:T(8,128)S(1)} %get-tuple-element.16, f32[64,128]{1,0:T(8,128)S(1)} %get-tuple-element.17, f32[256,64,128]{2,1,0:T(8,128)} %fusion.12, f32[256,64,128]{2,1,0:T(8,128)S(1)} %fusion.16, f32[256,64,128]{2,1,0:T(8,128)} %fusion.18, f32[256,64,128]{2,1,0:T(8,128)} %fusion.14), kind=kOutput, calls=%fused_computation.12 | convolution fusion | flops 413167616 | bytes 37814272 | tf_op jit(solution)/shard_map/an,cam->cnm/dot_general | solution.py:71
  274.2 16.1 %fusion.48 = bf16[256,32,128]{2,1,0:T(8,128)(2,1)S(1)} fusion(f32[256,128,32]{1,2,0:T(8,128)} %fusion.4, f32[64,128]{1,0:T(8,128)S(1)} %get-tuple-element.16, f32[64,128]{1,0:T(8,128)S(1)} %get-tuple-element.17, f32[256,64,128]{2,1,0:T(8,128)} %fusion.12, f32[256,64,128]{2,1,0:T(8,128)} %copy-done.3, f32[256,64,128]{2,1,0:T(8,128)} %fusion.18, ...), kind=kOutput, calls=%fused_computation.65 | convolution fusion | flops 416313344 | bytes 39911424 | tf_op jit(solution)/shard_map/an,cam->cnm/dot_general | solution.py:69
  293.6 3.9 reduce
  299.5 29.8 %all_to_all.39 = bf16[4,2,131072]{2,1,0:T(2,128)(2,1)S(1)} all-to-all(bf16[4,2,131072]{2,1,0:T(2,128)(2,1)} %reshape.75), channel_id=1, replica_groups=mesh['ctx'=4,'tp'=8] {'ctx'}, dimensions={0} | all-to-all | bytes 4194304 | tf_op jit(solution)/shard_map/all_to_all | solution.py:99
  329.4 3.3 reshape.76
  332.7 11.1 %copy.95 = f32[4,1024,1,256]{1,3,0,2:T(8,128)} copy(bf16[4,1024,1,256]{3,2,1,0:T(2,128)(2,1)} %bitcast.127) | data formatting | bytes 6291456 | tf_op jit(solution)/shard_map/convert_element_type | solution.py:102
  343.8 6.4 fusion.37
  350.2 27.0 %convolution_bitcast_fusion = f32[8192,1024]{0,1:T(8,128)} fusion(bf16[1024,1024]{0,1:T(8,128)(2,1)S(1)} %fusion.37, bf16[1024,8192]{1,0:T(8,128)(2,1)} %param.9), kind=kOutput, calls=%fused_computation | convolution fusion | flops 17179869184 | bytes 52428800 | tf_op jit(solution)/shard_map/dot_general | solution.py:105
  377.2 544.3 %reduce-scatter.2.cloned.1.call-done = f32[1024,1024]{0,1:T(8,128)} async-done(((f32[8192,1024]{0,1:T(8,128)}), f32[1024,1024]{0,1:T(8,128)}) %reduce-scatter.2.cloned.1.call-update) | async-done | bytes 4194320 | tf_op jit(solution)/shard_map/reduce_scatter | solution.py:104
  921.5 3.8 convert_bitcast_fusion
  (41 shorter events, 27.0 us)
Async XLA Ops:
  6.5 13.1 %copy-start.5 = (f32[3,3,1024]{2,1,0:T(4,128)S(1)}, f32[3,3,1024]{2,1,0:T(4,128)}, u32[]{:S(2)}) copy-start(f32[3,3,1024]{2,1,0:T(4,128)} %param.6) | copy-start | bytes 110596
  7.4 21.2 %collective-permute-start = (bf16[3,2,1024]{2,1,0:T(2,128)(2,1)S(1)}, bf16[3,2,1024]{2,1,0:T(2,128)(2,1)S(1)}, u32[]{:S(2)}, u32[]{:S(2)}) collective-permute-start(bf16[3,2,1024]{2,1,0:T(2,128)(2,1)S(1)} %slice.31), channel_id=1, source_target_pairs={{0,8},{8,16},{16,24},{1,9},{9,17},{17,25},{2,10},{10,18},{18,26},{... | collective-permute-start | bytes 36872 | tf_op jit(solution)/shard_map/ppermute | solution.py:14
  15.2 50.8 %all-to-all-start.1 = ((bf16[1024,4,256]{2,0,1:T(8,128)(2,1)}), bf16[1024,4,256]{2,0,1:T(8,128)(2,1)}, u32[]{:S(2)}, u32[]{:S(2)}) async-start(bf16[1024,4,256]{2,0,1:T(8,128)(2,1)} %copy.81), calls=%async_computation.1 | async-start | bytes 4194304 | tf_op jit(solution)/shard_map/all_to_all | solution.py:95
  58.1 4.5 copy-start
  66.0 56.0 %all-to-all-start = ((bf16[1024,4,256]{2,0,1:T(8,128)(2,1)}), bf16[1024,4,256]{2,0,1:T(8,128)(2,1)}, u32[]{:S(2)}, u32[]{:S(2)}) async-start(bf16[1024,4,256]{2,0,1:T(8,128)(2,1)} %copy.76), calls=%async_computation | async-start | bytes 4194304 | tf_op jit(solution)/shard_map/all_to_all | solution.py:94
  70.4 851.1 %reduce-scatter.2.cloned.1.call-start = ((), (), s32[]{:S(2)}) async-start(), calls=%async_computation.4 | async-start | bytes 37748736 | tf_op jit(solution)/shard_map/reduce_scatter | solution.py:104
  83.6 25.4 %copy-start.1 = (f32[256,64,128]{2,1,0:T(8,128)}, f32[256,64,128]{2,1,0:T(8,128)S(1)}, u32[]{:S(2)}) copy-start(f32[256,64,128]{2,1,0:T(8,128)S(1)} %get-tuple-element.10) | copy-start | bytes 25165828
  125.4 1.3 copy-start.4
  216.6 13.9 %copy-start.2 = (f32[256,64,128]{2,0,1:T(8,128)S(1)}, f32[256,64,128]{2,0,1:T(8,128)}, u32[]{:S(2)}) copy-start(f32[256,64,128]{2,0,1:T(8,128)} %get-tuple-element.5) | copy-start | bytes 25165828
  216.6 23.7 %slice-start = ((s8[8388608]{0:T(1024)(128)(4,1)}), s8[4194304]{0:T(1024)(128)(4,1)S(1)}, s32[]{:S(2)}) async-start(s8[8388608]{0:T(1024)(128)(4,1)} %bitcast.121), calls=%async_computation.5 | async-start | bytes 8388608
  230.6 29.0 %copy-start.3 = (f32[256,64,128]{2,1,0:T(8,128)}, f32[256,64,128]{2,1,0:T(8,128)S(1)}, u32[]{:S(2)}) copy-start(f32[256,64,128]{2,1,0:T(8,128)S(1)} %fusion.16) | copy-start | bytes 25165828
  230.6 9.7 %slice-start.1 = ((s8[8388608]{0:T(1024)(128)(4,1)}), s8[4194304]{0:T(1024)(128)(4,1)S(1)}, s32[]{:S(2)}) async-start(s8[8388608]{0:T(1024)(128)(4,1)} %bitcast.121), calls=%async_computation.6 | async-start | bytes 8388608
  329.4 14.4 %copy-start.6 = (f32[1024]{0:T(1024)S(1)}, f32[1024]{0:T(1024)}, u32[]{:S(2)}) copy-start(f32[1024]{0:T(1024)} %param.7) | copy-start | bytes 12292
Sparse Core Ops, SparseCore 0:
  377.4 544.1 reduce-scatter.1
where the time goes:
time: 941 us; the launch traced here: 933 us
  waiting for transfers between devices  544 us (58%)
  matrix products  236 us (25%)
  local copies, waits for them, and re-layouts  53.2 us (6%)
  other arithmetic  44.2 us (5%)
  blocking collectives  29.8 us (3%)
  between operations  14.1 us (1%)
  starting transfers between devices  11.5 us (1%)
    reduce_scatter x1, waiting for transfers between devices, on_device(): lax.psum_scatter(lax.dot_general(out_weight, gated, (((0,), (1,)), ((), (...  544 us
    dot_general x2, matrix products, forward(): jnp.einsum('cam,mk->cak', im_twist, cos_cols, precision=three_pass)  43.7 us
    all_to_all x1, blocking collectives, on_device(): lax.all_to_all(long_part, 'ctx', split_axis=0, concat_axis=1, tiled=True)  29.8 us
    dot_general x1, matrix products, on_device(): lax.dot_general(out_weight, gated, (((0,), (1,)), ((), ())), preferred_el...  27 us
    dot_general x2, matrix products, forward(): jnp.einsum('cam,mk->cak', re_twist, sin_cols, precision=three_pass)  25.6 us
    dot_general x2, matrix products, forward(): jnp.einsum('cam,mk->cak', im_twist, sin_cols, precision=three_pass)  25.5 us
    unnamed x26, local copies, waits for them, and re-layouts  25.4 us
    dot_general x2, matrix products, forward(): jnp.einsum('cam,mk->cak', re_twist, cos_cols, precision=three_pass)  25.1 us
  transfers between devices with their start and end apart: 4, of which 1 were waited for; matrix products, arithmetic and copies ran while one was open for 11% of the time, Pallas kernels for 0%

commit v1 on v0

--- a/solution.py
+++ b/solution.py
@@ -73,6 +73,62 @@
     return output_field.reshape(chan_count, seq_len).T
 
 
+def swapped(value, axis, bits):
+    count = lax.axis_size(axis)
+    return lax.ppermute(value, axis, [(source, source ^ bits) for source in range(count)])
+
+
+def column_block(weights, block, width):
+    return lax.dynamic_slice_in_dim(weights, block * width, width, axis=1)
+
+
+def swapped_weights(out_weight):
+    count = lax.axis_size("tp")
+    me = lax.axis_index("tp")
+    core = lax.rem(lax.axis_index("ctx"), 2)
+    rows, width = (out_weight.shape[0], out_weight.shape[1] // count)
+    half = rows // 2
+    blocks = {}
+    for high in range(count // 4):
+        for low in range(2):
+            wanted = me ^ (4 * high + low)
+            own = column_block(out_weight, wanted, width)
+            part = lax.dynamic_slice(out_weight, (core * half, (wanted ^ 2) * width), (half, width))
+            direct = swapped(part, "tp", 2)
+            shared = swapped(direct, "ctx", 1)
+            first = jnp.where(core == 0, direct, shared)
+            second = jnp.where(core == 0, shared, direct)
+            blocks[high, low] = (own, jnp.concatenate([first, second], axis=0))
+    return blocks
+
+
+def project(gated, blocks):
+    high_count = lax.axis_size("tp") // 4
+    pieces = 2
+    step = gated.shape[0] // pieces
+    results = []
+    for piece in range(pieces):
+        near = gated[piece * step : (piece + 1) * step]
+        far = swapped(near, "tp", 2)
+
+        def partial_sum(high, low):
+            own, other = blocks[high, low]
+            return jnp.dot(near, own, preferred_element_type=jnp.float32) + jnp.dot(
+                far, other, preferred_element_type=jnp.float32
+            )
+
+        arrived = []
+        for high in reversed(range(high_count)):
+            sent = swapped(partial_sum(high, 1).astype(jnp.bfloat16), "tp", 1)
+            total = partial_sum(high, 0) + sent.astype(jnp.float32)
+            if high:
+                arrived.append(swapped(total.astype(jnp.bfloat16), "tp", 4 * high))
+        for value in arrived:
+            total = total + value.astype(jnp.float32)
+        results.append(total.astype(jnp.bfloat16))
+    return jnp.concatenate(results, axis=0)
+
+
 def on_device(streams, conv_weight, skip_weight, long_filter, out_weight):
     tok_rows = streams.shape[1]
     chan_cols = streams.shape[2]
@@ -101,15 +157,7 @@
     gated = (
         (long_out.astype(jnp.float32) + skip_weight[None, :] * mixed_u.astype(jnp.float32)) * gating
     ).astype(jnp.bfloat16)
-    result = lax.psum_scatter(
-        lax.dot_general(
-            out_weight, gated, (((0,), (1,)), ((), ())), preferred_element_type=jnp.float32
-        ),
-        "tp",
-        scatter_dimension=0,
-        tiled=True,
-    ).T
-    return result.astype(jnp.bfloat16)
+    return project(gated, swapped_weights(out_weight))
 
 
 def solution(mesh):

time: 941 us -> 540 us (0.57)
  waiting for transfers between devices: 544 us -> 150 us
  blocking collectives: 29.8 us -> 0 us
  starting transfers between devices: 11.5 us -> 34 us
  between operations: 14.1 us -> 0.76 us
    reduce_scatter x1 -> x0, waiting for transfers between devices: 544 us -> none  [on_device(): lax.psum_scatter(lax.dot_general(out_weight, gated, (((0,), (1,)), ((), (...]
    ppermute x0 -> x16, waiting for transfers between devices: none -> 134 us  [swapped(): lax.ppermute(value, axis, [(source, source ^ bits) for source in range(co...]
    all_to_all x1 -> x0, blocking collectives: 29.8 us -> none  [on_device(): lax.all_to_all(long_part, 'ctx', split_axis=0, concat_axis=1, tiled=True)]
    ppermute x0 -> x16, starting transfers between devices: none -> 18 us  [swapped(): lax.ppermute(value, axis, [(source, source ^ bits) for source in range(co...]
    all_to_all x0 -> x1, waiting for transfers between devices: none -> 15.8 us  [on_device(): lax.all_to_all(long_part, 'ctx', split_axis=0, concat_axis=1, tiled=True)]
    unnamed x26 -> x46, local copies, waits for them, and re-layouts: 25.4 us -> 28 us
    dot_general x1 -> x16, matrix products: 27 us -> 24.7 us  [the longest x8 14.3 us: partial_sum(): jnp.dot(near, own, preferred_element_type=jnp.float32)]
  transfers between devices with their start and end apart: 4 -> 20, of which waited for: 1 -> 7; matrix products, arithmetic and copies ran while one was open for 11% -> 57% of each run, Pallas kernels for 0% -> 0%
where the time goes in v1:
time: 540 us; the launch traced here: 531 us
  matrix products  233 us (43%)
  waiting for transfers between devices  150 us (28%)
  local copies, waits for them, and re-layouts  60 us (11%)
  other arithmetic  52.9 us (10%)
  starting transfers between devices  34 us (6%)
    ppermute x16, waiting for transfers between devices, swapped(): lax.ppermute(value, axis, [(source, source ^ bits) for source in range(co...  134 us
    dot_general x2, matrix products, forward(): jnp.einsum('cam,mk->cak', im_twist, cos_cols, precision=three_pass)  43.4 us
    unnamed x46, local copies, waits for them, and re-layouts  28 us
    dot_general x2, matrix products, forward(): jnp.einsum('cam,mk->cak', re_twist, sin_cols, precision=three_pass)  26.1 us
    dot_general x2, matrix products, forward(): jnp.einsum('cam,mk->cak', im_twist, sin_cols, precision=three_pass)  25.1 us
    dot_general x2, matrix products, forward(): jnp.einsum('cam,mk->cak', re_twist, cos_cols, precision=three_pass)  25.1 us
    add x1, other arithmetic, on_device(): summed + conv_weight[:, lag_step, None, :] * extended[:, begin:begin + to...  18.4 us
    ppermute x16, starting transfers between devices, swapped(): lax.ppermute(value, axis, [(source, source ^ bits) for source in range(co...  18 us
  transfers between devices with their start and end apart: 20, of which 7 were waited for; matrix products, arithmetic and copies ran while one was open for 57% of the time, Pallas kernels for 0%

profile of v1, /device:TPU:0, one launch (start us, length us, event | category | flops | bytes accessed | tf_op | source)
XLA Modules:
  0.0 530.8 jit_solution(1803968874779727246)
XLA Ops:
  8.6 4.5 all-to-all-start.1
  21.9 8.6 %copy.75 = bf16[3,1024,1024]{1,2,0:T(8,128)(2,1)} copy(bf16[3,1024,1024]{2,1,0:T(8,128)(2,1)} %param.5) | data formatting | bytes 12582912 | tf_op args[0]
  30.9 11.0 %maximum_convert_fusion = f32[3,1026,1024]{1,2,0:T(8,128)} fusion(bf16[3,1024,1024]{1,2,0:T(8,128)(2,1)} %copy.75, bf16[3,2,1024]{1,2,0:T(8,128)(2,1)S(1)} %copy.74), kind=kLoop, calls=%fused_computation.47 | loop fusion | flops 12607488 | bytes 18911232 | tf_op jit(solution)/shard_map/convert_element_type | solution.py:137
  41.9 18.4 %fusion = f32[3,1024,1024]{1,2,0:T(8,128)S(1)} fusion(f32[3,1026,1024]{1,2,0:T(8,128)} %maximum_convert_fusion, f32[3,1024]{1,0:T(4,128)S(1)} %get-tuple-element.28, f32[3,1024]{1,0:T(4,128)S(1)} %get-tuple-element.29, f32[3,1024]{1,0:T(4,128)S(1)} %bitcast.137), kind=kLoop, calls=%fused_computation.1 | loop fusion | flops 15728640 | bytes 50368512 | tf_op jit(solution)/shard_map/add | solution.py:142
  60.3 4.6 copy-done
  69.3 4.7 all-to-all-start
  82.6 4.4 add_bitcast_fusion
  87.1 13.2 %fusion.24 = f32[256,64,128]{2,0,1:T(8,128)} fusion(f32[256,64,128]{2,1,0:T(8,128)S(1)} %get-tuple-element.9), kind=kOutput, calls=%fused_computation.35 | convolution fusion | flops 1610842112 | bytes 16777216 | tf_op jit(solution)/shard_map/cam,mk->cak/dot_general | solution.py:50
  100.3 12.5 %fusion.26 = f32[256,64,128]{2,0,1:T(8,128)} fusion(f32[256,64,128]{2,1,0:T(8,128)S(1)} %get-tuple-element.9), kind=kOutput, calls=%fused_computation.37 | convolution fusion | flops 1610842112 | bytes 16777216 | tf_op jit(solution)/shard_map/cam,mk->cak/dot_general | solution.py:47
  112.8 12.6 %fusion.22 = f32[256,64,128]{2,0,1:T(8,128)} fusion(f32[256,64,128]{2,1,0:T(8,128)S(1)} %get-tuple-element.10), kind=kOutput, calls=%fused_computation.33 | convolution fusion | flops 1610842112 | bytes 16777216 | tf_op jit(solution)/shard_map/cam,mk->cak/dot_general | solution.py:47
  132.7 5.8 %fusion.2 = (f32[256,64,128]{2,1,0:T(8,128)S(1)}, f32[256,64,128]{2,1,0:T(8,128)S(1)}) fusion(f32[256,128,64]{1,2,0:T(8,128)S(1)} %fusion.115, f32[64,128]{1,0:T(8,128)S(1)} %get-tuple-element.30, f32[64,128]{1,0:T(8,128)S(1)} %get-tuple-element.31, bf16[256,32,128]{2,1,0:T(8,128)(2,1)} %bitcast.128), kind=kOutput, calls=%fused_computation.7 | convolution fusion | flops 417361920 | bytes 27328512 | tf_op jit(solution)/shard_map/an,cnm->cam/dot_general | solution.py:43
  138.5 12.7 %fusion.28 = f32[256,64,128]{2,0,1:T(8,128)} fusion(f32[256,64,128]{2,1,0:T(8,128)S(1)} %get-tuple-element.8), kind=kOutput, calls=%fused_computation.39 | convolution fusion | flops 1610842112 | bytes 16777216 | tf_op jit(solution)/shard_map/cam,mk->cak/dot_general | solution.py:50
  151.2 12.5 %fusion.30 = f32[256,64,128]{2,0,1:T(8,128)} fusion(f32[256,64,128]{2,1,0:T(8,128)S(1)} %get-tuple-element.8), kind=kOutput, calls=%fused_computation.41 | convolution fusion | flops 1610842112 | bytes 16777216 | tf_op jit(solution)/shard_map/cam,mk->cak/dot_general | solution.py:47
  163.7 12.9 %fusion.32 = f32[256,64,128]{2,0,1:T(8,128)} fusion(f32[256,64,128]{2,1,0:T(8,128)S(1)} %get-tuple-element.7), kind=kOutput, calls=%fused_computation.43 | convolution fusion | flops 1610842112 | bytes 16777216 | tf_op jit(solution)/shard_map/cam,mk->cak/dot_general | solution.py:50
  176.6 12.5 %fusion.34 = f32[256,64,128]{2,0,1:T(8,128)} fusion(f32[256,64,128]{2,1,0:T(8,128)S(1)} %get-tuple-element.7), kind=kOutput, calls=%fused_computation.45 | convolution fusion | flops 1610842112 | bytes 16777216 | tf_op jit(solution)/shard_map/cam,mk->cak/dot_general | solution.py:47
  189.2 30.7 %multiply_subtract_fusion = (f32[256,64,128]{2,0,1:T(8,128)}, f32[256,64,128]{2,0,1:T(8,128)}) fusion(f32[256,64,128]{2,0,1:T(8,128)} %fusion.24, f32[256,64,128]{2,0,1:T(8,128)} %fusion.28, f32[256,64,128]{2,0,1:T(8,128)} %fusion.32, f32[256,64,128]{2,0,1:T(8,128)} %fusion.26, f32[256,64,128]{2,0,1:T(8,128)} %fusion.22, f32[256,64,128]{2,0,1:T(8,128)} %fusion.34, ...), kind=kOutput, calls=%fused_computation.20 | convolution fusion | flops 1631813632 | bytes 83886080 | tf_op jit(solution)/shard_map/cam,mk->cak/dot_general | solution.py:50
  219.8 14.0 %fusion.12 = f32[256,64,128]{2,1,0:T(8,128)S(1)} fusion(f32[256,64,128]{2,0,1:T(8,128)} %get-tuple-element.6), kind=kOutput, calls=%fused_computation.23 | convolution fusion | flops 1610842112 | bytes 16777216 | tf_op jit(solution)/shard_map/cak,mk->cam/dot_general | solution.py:64
  233.8 9.8 %fusion.14 = f32[256,64,128]{2,1,0:T(8,128)} fusion(f32[256,64,128]{2,0,1:T(8,128)S(1)} %copy-done.2), kind=kOutput, calls=%fused_computation.25 | convolution fusion | flops 1610842112 | bytes 16777216 | tf_op jit(solution)/shard_map/cak,mk->cam/dot_general | solution.py:61
  243.6 9.6 %fusion.16 = f32[256,64,128]{2,1,0:T(8,128)} fusion(f32[256,64,128]{2,0,1:T(8,128)S(1)} %bitcast.124), kind=kOutput, calls=%fused_computation.27 | convolution fusion | flops 1610842112 | bytes 16777216 | tf_op jit(solution)/shard_map/cak,mk->cam/dot_general | solution.py:64
  253.2 9.9 %fusion.18 = f32[256,64,128]{2,1,0:T(8,128)} fusion(f32[256,64,128]{2,0,1:T(8,128)S(1)} %bitcast.124), kind=kOutput, calls=%fused_computation.29 | convolution fusion | flops 1610842112 | bytes 16777216 | tf_op jit(solution)/shard_map/cak,mk->cam/dot_general | solution.py:61
  263.1 14.6 %fusion.4 = f32[256,128,32]{1,2,0:T(8,128)} fusion(f32[64,128]{1,0:T(8,128)S(1)} %get-tuple-element.30, f32[64,128]{1,0:T(8,128)S(1)} %get-tuple-element.31, f32[256,64,128]{2,1,0:T(8,128)S(1)} %fusion.12, f32[256,64,128]{2,1,0:T(8,128)} %fusion.16, f32[256,64,128]{2,1,0:T(8,128)} %fusion.18, f32[256,64,128]{2,1,0:T(8,128)} %fusion.14), kind=kOutput, calls=%fused_computation.11 | convolution fusion | flops 413167616 | bytes 37814272 | tf_op jit(solution)/shard_map/an,cam->cnm/dot_general | solution.py:71
  277.7 16.0 %fusion.48 = bf16[256,32,128]{2,1,0:T(8,128)(2,1)S(1)} fusion(f32[256,128,32]{1,2,0:T(8,128)} %fusion.4, f32[64,128]{1,0:T(8,128)S(1)} %get-tuple-element.30, f32[64,128]{1,0:T(8,128)S(1)} %get-tuple-element.31, f32[256,64,128]{2,1,0:T(8,128)} %copy-done.3, f32[256,64,128]{2,1,0:T(8,128)} %fusion.16, f32[256,64,128]{2,1,0:T(8,128)} %fusion.18, ...), kind=kOutput, calls=%fused_computation.64 | convolution fusion | flops 416313344 | bytes 39911424 | tf_op jit(solution)/shard_map/an,cam->cnm/dot_general | solution.py:69
  303.0 4.4 all-to-all-start.2
  317.5 15.8 %all-to-all-done.2 = bf16[4,2,131072]{2,1,0:T(2,128)(2,1)} async-done(((bf16[4,2,131072]{2,1,0:T(2,128)(2,1)}), bf16[4,2,131072]{2,1,0:T(2,128)(2,1)}, u32[]{:S(2)}, u32[]{:S(2)}) %all-to-all-start.2) | async-done | bytes 2097184 | tf_op jit(solution)/shard_map/all_to_all | solution.py:155
  333.2 5.0 reshape.76
  338.2 11.1 %copy.95 = f32[4,1024,1,256]{1,3,0,2:T(8,128)} copy(bf16[4,1024,1,256]{3,2,1,0:T(2,128)(2,1)} %bitcast.129) | data formatting | bytes 6291456 | tf_op jit(solution)/shard_map/convert_element_type | solution.py:158
  349.3 6.7 %fusion.37 = bf16[1024,1024]{0,1:T(8,128)(2,1)S(1)} fusion(f32[3,1024,1024]{1,2,0:T(8,128)} %copy-done, f32[4,1024,1,256]{1,3,0,2:T(8,128)} %copy.95, f32[1024]{0:T(1024)S(1)} %copy-done.12), kind=kLoop, calls=%fused_computation.50 | loop fusion | flops 7340032 | bytes 18878464 | tf_op jit(solution)/shard_map/convert_element_type | solution.py:159
  372.6 18.9 %collective-permute-done.1 = bf16[512,1024]{0,1:T(8,128)(2,1)S(1)} collective-permute-done((bf16[512,1024]{0,1:T(8,128)(2,1)S(1)}, bf16[512,1024]{0,1:T(8,128)(2,1)S(1)}, u32[]{:S(2)}, u32[]{:S(2)}) %collective-permute-start.1) | collective-permute-done | bytes 1048608 | tf_op jit(solution)/shard_map/ppermute | solution.py:78
  396.3 16.3 %collective-permute-done.13 = bf16[512,1024]{0,1:T(8,128)(2,1)S(1)} collective-permute-done((bf16[512,1024]{0,1:T(8,128)(2,1)S(1)}, bf16[512,1024]{0,1:T(8,128)(2,1)S(1)}, u32[]{:S(2)}, u32[]{:S(2)}) %collective-permute-start.13) | collective-permute-done | bytes 1048608 | tf_op jit(solution)/shard_map/ppermute | solution.py:78
  420.2 21.3 %collective-permute-done.11 = bf16[512,1024]{1,0:T(8,128)(2,1)S(1)} collective-permute-done((bf16[512,1024]{1,0:T(8,128)(2,1)S(1)}, bf16[512,1024]{1,0:T(8,128)(2,1)S(1)}, u32[]{:S(2)}, u32[]{:S(2)}) %collective-permute-start.11) | collective-permute-done | bytes 1048608 | tf_op jit(solution)/shard_map/ppermute | solution.py:78
  444.8 37.9 %collective-permute-done.15 = bf16[512,1024]{1,0:T(8,128)(2,1)S(1)} collective-permute-done((bf16[512,1024]{1,0:T(8,128)(2,1)S(1)}, bf16[512,1024]{1,0:T(8,128)(2,1)S(1)}, u32[]{:S(2)}, u32[]{:S(2)}) %collective-permute-start.15) | collective-permute-done | bytes 1048608 | tf_op jit(solution)/shard_map/ppermute | solution.py:78
  489.3 39.0 %collective-permute-done.16 = bf16[512,1024]{1,0:T(8,128)(2,1)S(1)} collective-permute-done((bf16[512,1024]{1,0:T(8,128)(2,1)S(1)}, bf16[512,1024]{1,0:T(8,128)(2,1)S(1)}, u32[]{:S(2)}, u32[]{:S(2)}) %collective-permute-start.16) | collective-permute-done | bytes 1048608 | tf_op jit(solution)/shard_map/ppermute | solution.py:78
  (115 shorter events, 98.3 us)
Async XLA Ops:
  0.8 29.7 %collective-permute-start = (bf16[3,2,1024]{2,1,0:T(2,128)(2,1)S(1)}, bf16[3,2,1024]{2,1,0:T(2,128)(2,1)S(1)}, u32[]{:S(2)}, u32[]{:S(2)}) collective-permute-start(bf16[3,2,1024]{2,1,0:T(2,128)(2,1)S(1)} %slice.37), channel_id=1, source_target_pairs={{0,8},{8,16},{16,24},{1,9},{9,17},{17,25},{2,10},{10,18},{18,26},{... | collective-permute-start | bytes 36872 | tf_op jit(solution)/shard_map/ppermute | solution.py:14
  8.6 60.7 %all-to-all-start.1 = ((bf16[1024,4,256]{2,0,1:T(8,128)(2,1)}), bf16[1024,4,256]{2,0,1:T(8,128)(2,1)}, u32[]{:S(2)}, u32[]{:S(2)}) async-start(bf16[1024,4,256]{2,0,1:T(8,128)(2,1)} %copy.81), calls=%async_computation.1 | async-start | bytes 4194304 | tf_op jit(solution)/shard_map/all_to_all | solution.py:151
  17.2 51.0 %collective-permute-start.2 = (bf16[512,1024]{1,0:T(8,128)(2,1)}, bf16[512,1024]{1,0:T(8,128)(2,1)}, u32[]{:S(2)}, u32[]{:S(2)}) collective-permute-start(bf16[512,1024]{1,0:T(8,128)(2,1)} %get-tuple-element.11), channel_id=1, source_target_pairs={{0,2},{1,3},{2,0},{3,1},{4,6},{5,7},{6,4},{7,5},{8,10},{9,11},{10,... | collective-permute-start | bytes 3145736 | tf_op jit(solution)/shard_map/ppermute | solution.py:78
  19.6 49.6 %collective-permute-start.4 = (bf16[512,1024]{1,0:T(8,128)(2,1)S(1)}, bf16[512,1024]{1,0:T(8,128)(2,1)}, u32[]{:S(2)}, u32[]{:S(2)}) collective-permute-start(bf16[512,1024]{1,0:T(8,128)(2,1)S(1)} %get-tuple-element.13), channel_id=1, source_target_pairs={{0,2},{1,3},{2,0},{3,1},{4,6},{5,7},{6,4},{7,5},{8,10},{9,11},{10,... | collective-permute-start | bytes 3145736 | tf_op jit(solution)/shard_map/ppermute | solution.py:78
  19.6 287.8 %collective-permute-start.9 = (bf16[512,1024]{1,0:T(8,128)(2,1)}, bf16[512,1024]{1,0:T(8,128)(2,1)}, u32[]{:S(2)}, u32[]{:S(2)}) collective-permute-start(bf16[512,1024]{1,0:T(8,128)(2,1)} %get-tuple-element.14), channel_id=1, source_target_pairs={{0,2},{1,3},{2,0},{3,1},{4,6},{5,7},{6,4},{7,5},{8,10},{9,11},{10,... | collective-permute-start | bytes 3145736 | tf_op jit(solution)/shard_map/ppermute | solution.py:78
  21.6 286.4 %collective-permute-start.7 = (bf16[512,1024]{1,0:T(8,128)(2,1)}, bf16[512,1024]{1,0:T(8,128)(2,1)}, u32[]{:S(2)}, u32[]{:S(2)}) collective-permute-start(bf16[512,1024]{1,0:T(8,128)(2,1)} %get-tuple-element.12), channel_id=1, source_target_pairs={{0,2},{1,3},{2,0},{3,1},{4,6},{5,7},{6,4},{7,5},{8,10},{9,11},{10,... | collective-permute-start | bytes 3145736 | tf_op jit(solution)/shard_map/ppermute | solution.py:78
  68.2 239.9 %collective-permute-start.3 = (bf16[512,1024]{1,0:T(8,128)(2,1)}, bf16[512,1024]{1,0:T(8,128)(2,1)}, u32[]{:S(2)}, u32[]{:S(2)}) collective-permute-start(bf16[512,1024]{1,0:T(8,128)(2,1)} %collective-permute-done.2), channel_id=1, source_target_pairs={{0,8},{8,0},{16,24},{24,16},{1,9},{9,1},{17,25},{25,17},{2,10},{10... | collective-permute-start | bytes 3145736 | tf_op jit(solution)/shard_map/ppermute | solution.py:78
  69.2 238.9 %collective-permute-start.5 = (bf16[512,1024]{1,0:T(8,128)(2,1)}, bf16[512,1024]{1,0:T(8,128)(2,1)}, u32[]{:S(2)}, u32[]{:S(2)}) collective-permute-start(bf16[512,1024]{1,0:T(8,128)(2,1)} %collective-permute-done.4), channel_id=1, source_target_pairs={{0,8},{8,0},{16,24},{24,16},{1,9},{9,1},{17,25},{25,17},{2,10},{10... | collective-permute-start | bytes 3145736 | tf_op jit(solution)/shard_map/ppermute | solution.py:78
  69.3 56.1 %all-to-all-start = ((bf16[1024,4,256]{2,0,1:T(8,128)(2,1)}), bf16[1024,4,256]{2,0,1:T(8,128)(2,1)}, u32[]{:S(2)}, u32[]{:S(2)}) async-start(bf16[1024,4,256]{2,0,1:T(8,128)(2,1)} %copy.76), calls=%async_computation | async-start | bytes 4194304 | tf_op jit(solution)/shard_map/all_to_all | solution.py:150
  87.0 25.8 %copy-start.1 = (f32[256,64,128]{2,1,0:T(8,128)}, f32[256,64,128]{2,1,0:T(8,128)S(1)}, u32[]{:S(2)}) copy-start(f32[256,64,128]{2,1,0:T(8,128)S(1)} %get-tuple-element.10) | copy-start | bytes 25165828
  219.8 14.0 %copy-start.2 = (f32[256,64,128]{2,0,1:T(8,128)S(1)}, f32[256,64,128]{2,0,1:T(8,128)}, u32[]{:S(2)}) copy-start(f32[256,64,128]{2,0,1:T(8,128)} %get-tuple-element.6) | copy-start | bytes 25165828
  219.8 23.8 %slice-start = ((s8[8388608]{0:T(1024)(128)(4,1)}), s8[4194304]{0:T(1024)(128)(4,1)S(1)}, s32[]{:S(2)}) async-start(s8[8388608]{0:T(1024)(128)(4,1)} %bitcast.123), calls=%async_computation.3 | async-start | bytes 8388608
  233.8 29.3 %copy-start.3 = (f32[256,64,128]{2,1,0:T(8,128)}, f32[256,64,128]{2,1,0:T(8,128)S(1)}, u32[]{:S(2)}) copy-start(f32[256,64,128]{2,1,0:T(8,128)S(1)} %fusion.12) | copy-start | bytes 25165828
  233.8 9.8 %slice-start.1 = ((s8[8388608]{0:T(1024)(128)(4,1)}), s8[4194304]{0:T(1024)(128)(4,1)S(1)}, s32[]{:S(2)}) async-start(s8[8388608]{0:T(1024)(128)(4,1)} %bitcast.123), calls=%async_computation.4 | async-start | bytes 8388608
  303.0 30.2 %all-to-all-start.2 = ((bf16[4,2,131072]{2,1,0:T(2,128)(2,1)}), bf16[4,2,131072]{2,1,0:T(2,128)(2,1)}, u32[]{:S(2)}, u32[]{:S(2)}) async-start(bf16[4,2,131072]{2,1,0:T(2,128)(2,1)} %reshape.75), calls=%async_computation.2 | async-start | bytes 4194304 | tf_op jit(solution)/shard_map/all_to_all | solution.py:155
  307.5 5.1 collective-permute-start.10
  308.0 5.5 %collective-permute-start.8 = (bf16[512,1024]{1,0:T(8,128)(2,1)}, bf16[512,1024]{1,0:T(8,128)(2,1)}, u32[]{:S(2)}, u32[]{:S(2)}) collective-permute-start(bf16[512,1024]{1,0:T(8,128)(2,1)} %collective-permute-done.7), channel_id=1, source_target_pairs={{0,8},{8,0},{16,24},{24,16},{1,9},{9,1},{17,25},{25,17},{2,10},{10... | collective-permute-start | bytes 3145736 | tf_op jit(solution)/shard_map/ppermute | solution.py:78
  338.2 11.1 %copy-start.12 = (f32[1024]{0:T(1024)S(1)}, f32[1024]{0:T(1024)}, u32[]{:S(2)}) copy-start(f32[1024]{0:T(1024)} %param.7) | copy-start | bytes 12292
  349.2 13.5 %slice-start.2 = ((s8[16777216]{0:T(1024)(128)(4,1)}), s8[4194304]{0:T(1024)(128)(4,1)S(1)}, s32[]{:S(2)}) async-start(s8[16777216]{0:T(1024)(128)(4,1)} %bitcast.135), calls=%async_computation.5 | async-start | bytes 8388608
  349.3 13.5 %slice-start.3 = ((s8[16777216]{0:T(1024)(128)(4,1)}), s8[4194304]{0:T(1024)(128)(4,1)S(1)}, s32[]{:S(2)}) async-start(s8[16777216]{0:T(1024)(128)(4,1)} %bitcast.135), calls=%async_computation.6 | async-start | bytes 8388608
  349.3 13.5 %slice-start.4 = ((s8[16777216]{0:T(1024)(128)(4,1)}), s8[4194304]{0:T(1024)(128)(4,1)S(1)}, s32[]{:S(2)}) async-start(s8[16777216]{0:T(1024)(128)(4,1)} %bitcast.135), calls=%async_computation.7 | async-start | bytes 8388608
  365.4 26.1 %collective-permute-start.1 = (bf16[512,1024]{0,1:T(8,128)(2,1)S(1)}, bf16[512,1024]{0,1:T(8,128)(2,1)S(1)}, u32[]{:S(2)}, u32[]{:S(2)}) collective-permute-start(bf16[512,1024]{0,1:T(8,128)(2,1)S(1)} %get-tuple-element.15), channel_id=1, source_target_pairs={{0,2},{1,3},{2,0},{3,1},{4,6},{5,7},{6,4},{7,5},{8,10},{9,11},{10,... | collective-permute-start | bytes 3145736 | tf_op jit(solution)/shard_map/ppermute | solution.py:78
  368.3 44.3 %collective-permute-start.13 = (bf16[512,1024]{0,1:T(8,128)(2,1)S(1)}, bf16[512,1024]{0,1:T(8,128)(2,1)S(1)}, u32[]{:S(2)}, u32[]{:S(2)}) collective-permute-start(bf16[512,1024]{0,1:T(8,128)(2,1)S(1)} %get-tuple-element.16), channel_id=1, source_target_pairs={{0,2},{1,3},{2,0},{3,1},{4,6},{5,7},{6,4},{7,5},{8,10},{9,11},{10,... | collective-permute-start | bytes 3145736 | tf_op jit(solution)/shard_map/ppermute | solution.py:78
  372.6 21.8 %copy-start.5 = (bf16[512,1024]{1,0:T(8,128)(2,1)S(1)}, bf16[512,1024]{1,0:T(8,128)(2,1)}, u32[]{:S(2)}) copy-start(bf16[512,1024]{1,0:T(8,128)(2,1)} %get-tuple-element.24) | copy-start | bytes 3145732
  392.8 95.7 %collective-permute-start.6 = (bf16[512,1024]{1,0:T(8,128)(2,1)S(1)}, bf16[512,1024]{1,0:T(8,128)(2,1)S(1)}, u32[]{:S(2)}, u32[]{:S(2)}) collective-permute-start(bf16[512,1024]{1,0:T(8,128)(2,1)S(1)} %add_convert_fusion.7), channel_id=1, source_target_pairs={{0,1},{1,0},{2,3},{3,2},{4,5},{5,4},{6,7},{7,6},{8,9},{9,8},{10,11... | collective-permute-start | bytes 3145736 | tf_op jit(solution)/shard_map/ppermute | solution.py:78
  395.7 45.7 %collective-permute-start.11 = (bf16[512,1024]{1,0:T(8,128)(2,1)S(1)}, bf16[512,1024]{1,0:T(8,128)(2,1)S(1)}, u32[]{:S(2)}, u32[]{:S(2)}) collective-permute-start(bf16[512,1024]{1,0:T(8,128)(2,1)S(1)} %add_convert_fusion.6), channel_id=1, source_target_pairs={{0,1},{1,0},{2,3},{3,2},{4,5},{5,4},{6,7},{7,6},{8,9},{9,8},{10,11... | collective-permute-start | bytes 3145736 | tf_op jit(solution)/shard_map/ppermute | solution.py:78
  413.9 75.4 %collective-permute-start.14 = (bf16[512,1024]{1,0:T(8,128)(2,1)S(1)}, bf16[512,1024]{1,0:T(8,128)(2,1)S(1)}, u32[]{:S(2)}, u32[]{:S(2)}) collective-permute-start(bf16[512,1024]{1,0:T(8,128)(2,1)S(1)} %add_convert_fusion.3), channel_id=1, source_target_pairs={{0,1},{1,0},{2,3},{3,2},{4,5},{5,4},{6,7},{7,6},{8,9},{9,8},{10,11... | collective-permute-start | bytes 3145736 | tf_op jit(solution)/shard_map/ppermute | solution.py:78
  416.8 65.9 %collective-permute-start.15 = (bf16[512,1024]{1,0:T(8,128)(2,1)S(1)}, bf16[512,1024]{1,0:T(8,128)(2,1)S(1)}, u32[]{:S(2)}, u32[]{:S(2)}) collective-permute-start(bf16[512,1024]{1,0:T(8,128)(2,1)S(1)} %add_convert_fusion.2), channel_id=1, source_target_pairs={{0,1},{1,0},{2,3},{3,2},{4,5},{5,4},{6,7},{7,6},{8,9},{9,8},{10,11... | collective-permute-start | bytes 3145736 | tf_op jit(solution)/shard_map/ppermute | solution.py:78
  442.1 43.9 %copy-start.6 = (bf16[512,1024]{1,0:T(8,128)(2,1)S(1)}, bf16[512,1024]{1,0:T(8,128)(2,1)}, u32[]{:S(2)}) copy-start(bf16[512,1024]{1,0:T(8,128)(2,1)} %get-tuple-element.34) | copy-start | bytes 3145732
  442.1 43.9 %copy-start.7 = (bf16[512,1024]{1,0:T(8,128)(2,1)S(1)}, bf16[512,1024]{1,0:T(8,128)(2,1)}, u32[]{:S(2)}) copy-start(bf16[512,1024]{1,0:T(8,128)(2,1)} %get-tuple-element.35) | copy-start | bytes 3145732
  442.1 46.5 %collective-permute-start.12 = (bf16[512,1024]{1,0:T(8,128)(2,1)S(1)}, bf16[512,1024]{1,0:T(8,128)(2,1)S(1)}, u32[]{:S(2)}, u32[]{:S(2)}) collective-permute-start(bf16[512,1024]{1,0:T(8,128)(2,1)S(1)} %add_convert_fusion.5), channel_id=1, source_target_pairs={{0,4},{1,5},{2,6},{3,7},{4,0},{5,1},{6,2},{7,3},{8,12},{9,13},{10,... | collective-permute-start | bytes 3145736 | tf_op jit(solution)/shard_map/ppermute | solution.py:78
  483.4 45.0 %collective-permute-start.16 = (bf16[512,1024]{1,0:T(8,128)(2,1)S(1)}, bf16[512,1024]{1,0:T(8,128)(2,1)S(1)}, u32[]{:S(2)}, u32[]{:S(2)}) collective-permute-start(bf16[512,1024]{1,0:T(8,128)(2,1)S(1)} %add_convert_fusion.1), channel_id=1, source_target_pairs={{0,4},{1,5},{2,6},{3,7},{4,0},{5,1},{6,2},{7,3},{8,12},{9,13},{10,... | collective-permute-start | bytes 3145736 | tf_op jit(solution)/shard_map/ppermute | solution.py:78
  (7 other events, 29.1 us)
